TPU v7x, 32 devices: a whole 2x2x4 slice. The times are simulated.
32 devices in a mesh: state: 8 (over y, x, core), mesh: 4 (over z).
Axes of the slice: x: 2, y: 2, z: 4, core: 2. Of those that a mesh axis runs over, the one named last changes fastest.
Arguments:
- states_in: float32 [5508, 4096], P('mesh', 'state'), may hold values from -6 to 6
- rotation: float32 [4096, 4096], P(None, 'state'), may hold values from -0.09375 to 0.09375
- stiffness: float32 [4, 729, 729], P('mesh'), as said below
- potential: float32 [5508], P('mesh'), may hold values from -1 to 1
- cell_nodes: int32 [8, 729], P('mesh'), may hold values from 0 to 1376, as said below
- shared_rows: int32 [16, 153], P('mesh'), may hold values from 0 to 1376, as said below
- shared_count: int32 [4, 4], P('mesh'), may hold values from 0 to 153, as said below
Outputs:
- filtered: float32 [5508, 4096], P('mesh', 'state')
Inputs may be any that keep to these rules, and one draw needn't show every extreme that they name: `cell_nodes`: each partition's 2 cells name its 1377 local nodes as a row of hexahedral cells of order 8 sharing faces; every local node is named by some cell. `shared_rows`: used rows name the partition's nodes on the face toward the partner, in the same geometric order as the partner's matching list; rows beyond the count name arbitrary local nodes. `shared_count`: count s of partition p equals count s ^ 1 of its partner; for s = 0, 1 it is 0 or from 40 to 81, for s = 2, 3 it is 0 or from 76 to 153; it is 0 where the partner lies outside the G by G grid; count 2 of partition 0 is 153. `stiffness`: symmetric with a diagonal of 1 to 3.
All inputs are finite; a program needn't handle non-finite values.
Results may differ from a plain program's by a relative error of at most 0.0001.
Values sent between devices are 32-bit elements; how exact they have to be, the bound alone decides.
A program may use at most 128 MiB of HBM per device.

v0:
```python
import functools
import math

import jax
import jax.numpy as jnp
from jax import lax
from jax.experimental import pallas as pl
from jax.experimental.pallas import tpu as pltpu
from jax.sharding import PartitionSpec as P

center_shift = 3.0
half_width = 4.0
f32 = jnp.float32
bf16 = jnp.bfloat16
MESH = pl.DeviceIdType.MESH


def from_behind(value, axis, steps):
    count = lax.axis_size(axis)
    first, last = (max(0, -steps), min(count, count - steps))
    return lax.ppermute(value, axis, [(source, source + steps) for source in range(first, last)])


def matmul(left, right):
    return jnp.dot(left, right, precision=lax.Precision.HIGHEST, preferred_element_type=jnp.float32)


def per_device(states_in, rotation, stiffness, potential, cell_nodes, shared_rows, shared_count):
    block_cols = states_in.shape[1]
    rotated = matmul(lax.all_gather(states_in, "state", axis=1, tiled=True), rotation)
    grid_side = math.isqrt(lax.axis_size("mesh"))
    row_mask = (jnp.arange(shared_rows.shape[1])[None, :] < shared_count[0][:, None]).astype(
        jnp.float32
    )

    def trade(values, send_slot, recv_slot, offset):
        block = values[shared_rows[send_slot]] * row_mask[send_slot][:, None]
        arrived = from_behind(block, "mesh", offset)
        return arrived * row_mask[recv_slot][:, None]

    def operator(field):
        gathered = field[cell_nodes]
        product = jnp.einsum("ij,cjs->cis", stiffness[0], gathered, precision=lax.Precision.HIGHEST)
        local = (
            jnp.zeros_like(field).at[cell_nodes.reshape(-1)].add(product.reshape(-1, block_cols))
        )
        from_next = trade(local, 1, 0, -grid_side)
        from_prev = trade(local, 0, 1, grid_side)
        sectioned = local.at[shared_rows[0]].add(from_next).at[shared_rows[1]].add(from_prev)
        from_right = trade(sectioned, 3, 2, -1)
        from_left = trade(sectioned, 2, 3, 1)
        assembled = sectioned.at[shared_rows[2]].add(from_right).at[shared_rows[3]].add(from_left)
        return assembled + potential[:, None] * field

    current = (operator(rotated) - center_shift * rotated) / half_width
    applied = operator(current)
    following = 2.0 * (applied - center_shift * current) / half_width - rotated
    return following


def up(size, unit):
    return -(-size // unit) * unit


def dot(left, right):
    return jnp.dot(left, right, preferred_element_type=f32)


def split(value):
    high = value.astype(bf16)
    return high, (value - high.astype(f32)).astype(bf16)


def dot3(lh, ll, rh, rl):
    return dot(lh, rh) + (dot(lh, rl) + dot(ll, rh))


def dot2(left, rh, rl):
    return dot(left, rh) + dot(left, rl)


def one_hot(left, right):
    return jnp.where(left == right, 1.0, 0.0).astype(bf16)


def one_hot_used(left, right):
    return jnp.where((left == right) & (left >= 0), 1.0, 0.0).astype(bf16)


def to_column(row):
    spread = jnp.broadcast_to(row.astype(f32), (128, row.shape[1]))
    return jnp.transpose(spread)[:, 0:1].astype(jnp.int32)


def kernel(
    grid_side, near_rows, far_rows,
    x_ref, rot_ref, k_ref, pot_ref, cells_ref, lists_ref, count_ref, out_ref,
    g, rbuf, c1, kh, kl, pick, same, gh, gl, ph, pl_, bv, rh, rl,
    pot, crow, crep, ccol, dcol, near_row, far_row, near_col, far_col,
    put_a, got_a, put_b, got_b,
    g_send, g_recv, e_send, e_recv, r_sem,
):
    nodes = x_ref.shape[0]
    n_pad, cols = c1.shape
    half = cols // 2
    n_send = up(nodes, 8)
    mid = n_pad // 2
    tile = n_pad // 4
    cells, npc = cells_ref.shape
    stride = kh.shape[0]
    side = 256
    me = lax.axis_index("state")
    part = lax.axis_index("mesh")

    def flip(index, bit):
        return index + bit * (1 - 2 * (index // bit % 2))

    sib, xs, ys = flip(me, 1), flip(me, 2), flip(me, 4)
    ds = flip(xs, 4)
    pair_a, pair_b = flip(part, grid_side), flip(part, 1)
    top, low = pl.ds(0, mid), pl.ds(mid, n_send - mid)
    whole = pl.ds(0, n_send)

    barrier = pltpu.get_barrier_semaphore()
    for target in ({"state": sib}, {"state": xs}, {"state": ys}, {"mesh": pair_a}, {"mesh": pair_b}):
        pl.semaphore_signal(barrier, inc=1, device_id=target, device_id_type=MESH)

    def load_rotation(phase):
        copies = []
        for block in range(rbuf.shape[0]):
            copy = pltpu.make_async_copy(
                rot_ref.at[pl.ds(block * cols + phase * half, half)], rbuf.at[block], r_sem.at[block]
            )
            copy.start()
            copies.append(copy)
        return copies

    rotation_copies = load_rotation(0)
    last = nodes // 8 * 8
    for phase in range(2):
        g[phase, me, pl.ds(last, n_pad - last), :] = jnp.zeros((n_pad - last, half), f32)
        g[phase, me, pl.ds(0, nodes), :] = x_ref[:, phase * half : (phase + 1) * half]
    pl.semaphore_wait(barrier, 5)

    def send(phase, number, owner, rows, target):
        return pltpu.make_async_remote_copy(
            src_ref=g.at[phase, owner, rows],
            dst_ref=g.at[phase, owner, rows],
            send_sem=g_send.at[phase, number],
            recv_sem=g_recv.at[phase, number],
            device_id={"state": target},
            device_id_type=MESH,
        )

    def plan(phase):
        return [
            send(phase, 0, me, top, xs),
            send(phase, 1, me, low, xs),
            send(phase, 2, ys, low, xs),
            send(phase, 3, me, low, ys),
            send(phase, 4, me, top, ys),
            send(phase, 5, xs, top, ys),
            send(phase, 6, me, whole, sib),
            send(phase, 7, xs, top, sib),
            send(phase, 8, xs, low, sib),
            send(phase, 9, ys, low, sib),
            send(phase, 10, ys, top, sib),
            send(phase, 11, ds, low, sib),
            send(phase, 12, ds, top, sib),
        ]

    plans = [plan(0), plan(1)]

    def begin(phase, *numbers):
        for number in numbers:
            plans[phase][number].start()

    def pass_on(phase, number, *onward):
        plans[phase][number].wait_recv()
        begin(phase, *onward)

    def pass_first(phase):
        pass_on(phase, 3, 2, 9)
        pass_on(phase, 0, 5, 7)

    def pass_second(phase):
        pass_on(phase, 1, 8)
        pass_on(phase, 4, 10)

    def pass_third(phase):
        pass_on(phase, 2, 11)
        pass_on(phase, 5, 12)

    def arrived(phase, *numbers):
        for number in numbers:
            plans[phase][number].wait_recv()

    begin(0, 0, 3, 6)

    def tiles(count, size, body):
        def step(index, carry):
            body(pl.ds(pl.multiple_of(index * size, 32), size))
            return carry

        lax.fori_loop(0, count // size, step, 0)

    pot[...] = jnp.zeros(pot.shape, f32)
    pot[:, 0:nodes] = pot_ref[...]
    crow[...] = jnp.full(crow.shape, -1, jnp.int32)
    for cell in range(cells):
        crow[:, cell * stride : cell * stride + npc] = cells_ref[cell : cell + 1, :]
    near_row[...] = jnp.full(near_row.shape, -1, jnp.int32)
    far_row[...] = jnp.full(far_row.shape, -1, jnp.int32)
    for row_ref, offset, place in ((near_row, 0, part // grid_side), (far_row, 2, part % grid_side)):
        size = near_rows if row_ref is near_row else far_rows
        ids = lax.broadcasted_iota(jnp.int32, (1, size), 1)
        second = place == 1
        listed = jnp.where(
            second, lists_ref[offset + 1 : offset + 2, 0:size], lists_ref[offset : offset + 1, 0:size]
        )
        count = jnp.where(second, count_ref[0, offset + 1], count_ref[0, offset])
        row_ref[:, 0:size] = jnp.where(ids < count, listed, -1)
    near_col[...] = to_column(near_row[...])[0 : near_col.shape[0]]
    far_col[...] = to_column(far_row[...])[0 : far_col.shape[0]]
    ccol[...] = to_column(crow[...])

    for first in range(0, stride, cols):
        width = min(cols, stride - first)
        used = min(npc - first, width)
        out_ref[0:stride, 0:width] = jnp.zeros((stride, width), f32)
        out_ref[0:npc, 0:used] = k_ref[0, :, first : first + used]
        span = slice(first, first + width)
        kh[:, span], kl[:, span] = split(out_ref[0:stride, 0:width])

    def pick_body(rows):
        ids = lax.broadcasted_iota(jnp.int32, (side, n_pad), 1)
        here = ccol[rows, :] == ids
        pick[rows, :] = jnp.where(here, 1.0, 0.0).astype(bf16)
        dcol[rows, :] = jnp.sum(jnp.where(here, pot[...], 0.0), axis=1, keepdims=True) - center_shift

    tiles(cells * stride, side, pick_body)
    crep[...] = crow[...]
    pairs = [(one, two) for one in range(cells) for two in range(cells) if one != two]
    for index, (one, two) in enumerate(pairs):
        left = ccol[one * stride : (one + 1) * stride, :]
        span = slice(two * stride, (two + 1) * stride)
        both = one_hot_used(left, crow[:, span])
        same[index] = both
        if one < two:
            taken = jnp.max(both.astype(f32), axis=0, keepdims=True)
            crep[:, span] = jnp.where(taken > 0.5, -1, crep[:, span])

    begin(0, 1, 4)

    def rotate(phase, owner, total, fresh=False):
        rh[...], rl[...] = split(rbuf[owner])

        def body(rows):
            high, rest = split(g[phase, owner, rows, :])
            value = dot3(high, rest, rh[...], rl[...])
            total[rows, :] = value if fresh else total[rows, :] + value

        tiles(n_pad, tile, body)

    def trade(field, number, which):
        put, got, pair = ((put_a, got_a, pair_a), (put_b, got_b, pair_b))[which]
        slot = 2 * field + number
        return pltpu.make_async_remote_copy(
            src_ref=put.at[slot],
            dst_ref=got.at[slot],
            send_sem=e_send.at[which, slot],
            recv_sem=e_recv.at[which, slot],
            device_id={"mesh": pair},
            device_id_type=MESH,
        )

    def enter(bank, read):
        def split_body(rows):
            ph[bank, rows, :], pl_[bank, rows, :] = split(read(rows))

        tiles(n_pad, tile, split_body)

        def body(rows):
            gh[bank, rows, :] = dot(pick[rows, :], ph[bank, 0:n_pad, :]).astype(bf16)
            gl[bank, rows, :] = dot(pick[rows, :], pl_[bank, 0:n_pad, :]).astype(bf16)

        tiles(cells * stride, side, body)

    def product(bank, field, number):
        for cell in range(cells):
            span = slice(cell * stride, (cell + 1) * stride)

            def body(rows):
                value = dot3(kh[rows, :], kl[rows, :], gh[bank, span, :], gl[bank, span, :])
                here = pl.ds(pl.multiple_of(rows.start + cell * stride, 32), side)
                ph[bank, here, :], pl_[bank, here, :] = split(value)
                held = gh[bank, here, :].astype(f32) + gl[bank, here, :].astype(f32)
                bv[bank, here, :] = value + dcol[here, :] * held

            tiles(stride, side, body)
        slot = 2 * field + number
        for put, col in ((put_a, near_col), (put_b, far_col)):
            put[slot] = dot2(one_hot_used(col[...], crow[...]), ph[bank], pl_[bank])
            if put is put_a:
                trade(field, number, 0).start()

    def couple(bank):
        for index, (one, two) in enumerate(pairs):
            span = slice(two * stride, (two + 1) * stride)

            def body(rows):
                here = pl.ds(pl.multiple_of(rows.start + one * stride, 32), side)
                value = dot2(same[index, rows, :], ph[bank, span, :], pl_[bank, span, :])
                bv[bank, here, :] = bv[bank, here, :] + value

            tiles(stride, side, body)

    def link(field, number):
        slot = 2 * field + number
        trade(field, number, 0).wait_recv()
        corner = one_hot_used(far_col[...], near_row[:, 0 : near_col.shape[0]])
        put_b[slot] = put_b[slot] + dot2(corner, *split(got_a[slot]))
        trade(field, number, 1).start()

    def finish(bank, field, number):
        slot = 2 * field + number
        trade(field, number, 1).wait_recv()
        near_high, near_rest = split(got_a[slot])
        far_high, far_rest = split(got_b[slot])

        def body(rows):
            near = one_hot_used(ccol[rows, :], near_row[:, 0 : near_col.shape[0]])
            far = one_hot_used(ccol[rows, :], far_row[:, 0 : far_col.shape[0]])
            value = bv[bank, rows, :] + dot2(near, near_high, near_rest)
            value = value + dot2(far, far_high, far_rest)
            gh[bank, rows, :], gl[bank, rows, :] = split(value * (1.0 / half_width))

        tiles(cells * stride, side, body)

    def leave(bank, write):
        def body(rows):
            ids = lax.broadcasted_iota(jnp.int32, (tile, crep.shape[1]), 0) + rows.start
            write(rows, dot2(one_hot(ids, crep[...]), gh[bank], gl[bank]))

        tiles(n_pad, tile, body)

    enter(0, lambda rows: g[1, me, rows, :])
    product(0, 0, 0)
    couple(0)
    for copy in rotation_copies:
        copy.wait()
    rotate(0, me, c1, fresh=True)
    link(0, 0)
    arrived(0, 6)
    rotate(0, sib, c1)
    finish(0, 0, 0)
    product(0, 0, 1)
    couple(0)
    pass_first(0)
    link(0, 1)
    finish(0, 0, 1)

    def leave_half(rows, value):
        g[1, me, rows, :] = 2.0 * value - g[1, me, rows, :]

    leave(0, leave_half)
    begin(1, 0, 3, 6)
    pass_second(0)
    rotate(0, xs, c1)
    rotate(0, ys, c1)
    arrived(0, 7, 8)
    rotate(0, flip(xs, 1), c1)
    arrived(0, 9, 10)
    rotate(0, flip(ys, 1), c1)
    pass_third(0)
    begin(1, 1, 4)
    rotate(0, ds, c1)
    arrived(0, 11, 12)
    rotate(0, flip(ds, 1), c1)
    rotation_copies = load_rotation(1)
    c1[pl.ds(n_send, n_pad - n_send), :] = jnp.zeros((n_pad - n_send, cols), f32)

    spans = [slice(0, half), slice(half, cols)]

    for bank in range(2):
        enter(bank, lambda rows: c1[rows, spans[bank]])
        product(bank, bank + 1, 0)
    for bank in range(2):
        couple(bank)
        link(bank + 1, 0)
    for copy in rotation_copies:
        copy.wait()
    rotate(1, me, out_ref, fresh=True)
    pass_first(1)
    for bank in range(2):
        finish(bank, bank + 1, 0)
        product(bank, bank + 1, 1)
    for bank in range(2):
        couple(bank)
        link(bank + 1, 1)
    arrived(1, 6)
    rotate(1, sib, out_ref)
    pass_second(1)
    for bank in range(2):
        finish(bank, bank + 1, 1)

        def leave_whole(rows, value):
            span = spans[bank]
            out_ref[rows, span] = out_ref[rows, span] + (2.0 * value - c1[rows, span])

        leave(bank, leave_whole)
    rotate(1, xs, out_ref)
    rotate(1, ys, out_ref)
    pass_third(1)
    arrived(1, 7, 8)
    rotate(1, flip(xs, 1), out_ref)
    arrived(1, 9, 10)
    rotate(1, flip(ys, 1), out_ref)
    rotate(1, ds, out_ref)
    arrived(1, 11, 12)
    rotate(1, flip(ds, 1), out_ref)
    for moves in plans:
        for move in moves:
            move.wait_send()
    for field in range(3):
        for number in range(2):
            for which in range(2):
                trade(field, number, which).wait_send()


def square_device(states_in, rotation, stiffness, potential, cell_nodes, shared_rows, shared_count):
    nodes, cols = states_in.shape
    half = cols // 2
    blocks = lax.axis_size("state")
    n_pad = up(nodes, 128)
    cells, npc = cell_nodes.shape
    stride = up(npc, 256)
    side = round(npc ** (1 / 3))
    near_rows, far_rows = side * side, shared_rows.shape[1]
    near, far = up(near_rows, 32), up(far_rows, 32)
    grid_side = math.isqrt(lax.axis_size("mesh"))
    vmem = pl.BlockSpec(memory_space=pltpu.VMEM)
    smem = pl.BlockSpec(memory_space=pltpu.SMEM)
    scratch = [
        pltpu.VMEM((2, blocks, n_pad, half), f32),
        pltpu.VMEM((blocks, half, cols), f32),
        pltpu.VMEM((n_pad, cols), f32),
        pltpu.VMEM((stride, stride), bf16),
        pltpu.VMEM((stride, stride), bf16),
        pltpu.VMEM((cells * stride, n_pad), bf16),
        pltpu.VMEM((cells * (cells - 1), stride, stride), bf16),
        pltpu.VMEM((2, cells * stride, half), bf16),
        pltpu.VMEM((2, cells * stride, half), bf16),
        pltpu.VMEM((2, cells * stride, half), bf16),
        pltpu.VMEM((2, cells * stride, half), bf16),
        pltpu.VMEM((2, cells * stride, half), f32),
        pltpu.VMEM((half, cols), bf16),
        pltpu.VMEM((half, cols), bf16),
        pltpu.VMEM((1, n_pad), f32),
        pltpu.VMEM((1, cells * stride), jnp.int32),
        pltpu.VMEM((1, cells * stride), jnp.int32),
        pltpu.VMEM((cells * stride, 1), jnp.int32),
        pltpu.VMEM((cells * stride, 1), f32),
        pltpu.VMEM((1, up(near, 128)), jnp.int32),
        pltpu.VMEM((1, up(far, 128)), jnp.int32),
        pltpu.VMEM((near, 1), jnp.int32),
        pltpu.VMEM((far, 1), jnp.int32),
        pltpu.VMEM((6, near, half), f32),
        pltpu.VMEM((6, near, half), f32),
        pltpu.VMEM((6, far, half), f32),
        pltpu.VMEM((6, far, half), f32),
        pltpu.SemaphoreType.DMA((2, 13)),
        pltpu.SemaphoreType.DMA((2, 13)),
        pltpu.SemaphoreType.DMA((2, 6)),
        pltpu.SemaphoreType.DMA((2, 6)),
        pltpu.SemaphoreType.DMA((blocks,)),
    ]
    padded = pl.pallas_call(
        functools.partial(kernel, grid_side, near_rows, far_rows),
        out_shape=jax.ShapeDtypeStruct((n_pad, cols), f32),
        in_specs=[vmem, pl.BlockSpec(memory_space=pl.ANY), vmem, vmem, vmem, vmem, smem],
        out_specs=vmem,
        scratch_shapes=scratch,
        compiler_params=pltpu.CompilerParams(
            collective_id=0, has_side_effects=True, vmem_limit_bytes=64 * 1024 * 1024
        ),
    )(
        states_in, rotation, stiffness, potential[None, :], cell_nodes, shared_rows, shared_count
    )
    return padded[:nodes]


def solution(mesh):
    squares = mesh.shape["state"] == 2 * 2 * 2 and mesh.shape["mesh"] == 2 * 2
    return jax.shard_map(
        square_device if squares else per_device,
        mesh=mesh,
        in_specs=(
            P("mesh", "state"),
            P(None, "state"),
            P("mesh", None, None),
            P("mesh"),
            P("mesh", None),
            P("mesh", None),
            P("mesh", None),
        ),
        out_specs=P("mesh", "state"),
        check_vma=False,
    )
```

profile of v0, /device:TPU:0, one launch (start us, length us, event | category | flops | bytes accessed | tf_op | source)
XLA Modules:
  0.0 139.5 jit_solution(7951396305200338266)
XLA Ops:
  0.0 1.3 broadcast_in_dim.3.pot_ref
  1.3 3.1 %copy.8.k_ref = f32[1,729,729]{2,1,0:T(8,128)} copy(f32[1,729,729]{2,0,1:T(1,128)} %param.9) | data formatting | bytes 4251528 | tf_op args[2]
  4.4 131.4 %shard_map.73 = f32[1408,512]{1,0:T(8,128)} custom-call(f32[1377,512]{1,0:T(8,128)} %x_ref.1, f32[4096,512]{1,0:T(8,128)} %rot_ref.1, f32[1,729,729]{2,1,0:T(8,128)} %copy.8.k_ref, f32[1,1377]{1,0:T(1,128)} %broadcast_in_dim.3.pot_ref, s32[2,729]{1,0:T(2,128)} %cells_ref.1, s32[4,153]{1,0:T(4,128)} %lists_ref.1, s32[1,4]{1,0:T(1,128)} %count_ref.1), custom_call_target="tpu_custom_call" | custom-call | tf_op jit(solution)/shard_map/pallas_call | solution.py:478
  135.8 3.6 %slice.3 = f32[1377,512]{1,0:T(8,128)} slice(f32[1408,512]{1,0:T(8,128)} %shard_map.73), slice={[0:1377], [0:512]} | slice | bytes 5640192 | tf_op jit(solution)/shard_map/slice | solution.py:490
where the time goes:
time: 140 us; the launch traced here: 139 us
  Pallas kernels  131 us (94%)
  local copies, waits for them, and re-layouts  8.07 us (6%)
    pallas_call x1, Pallas kernels, square_device(): pl.pallas_call(functools.partial(kernel, grid_side, near_rows, far_rows),...  131 us
    slice x1, local copies, waits for them, and re-layouts, square_device(): return padded[:nodes]  3.63 us
    unnamed x1, local copies, waits for them, and re-layouts  3.15 us

commit v1 on v0

--- a/solution.py
+++ b/solution.py
@@ -95,9 +95,9 @@
 def kernel(
     grid_side, near_rows, far_rows,
     x_ref, rot_ref, k_ref, pot_ref, cells_ref, lists_ref, count_ref, out_ref,
-    g, rbuf, c1, kh, kl, pick, same, gh, gl, ph, pl_, bv, rh, rl,
+    g, rbuf, c1, kh, kl, pick, same, gh, gl, ph, pl_, bv, r3,
     pot, crow, crep, ccol, dcol, near_row, far_row, near_col, far_col,
-    put_a, got_a, put_b, got_b,
+    half_put_a, half_got_a, half_put_b, half_got_b, put_a, got_a, put_b, got_b,
     g_send, g_recv, e_send, e_recv, r_sem,
 ):
     nodes = x_ref.shape[0]
@@ -105,10 +105,10 @@
     half = cols // 2
     n_send = up(nodes, 8)
     mid = n_pad // 2
-    tile = n_pad // 4
+    tile = n_pad // 2
     cells, npc = cells_ref.shape
     stride = kh.shape[0]
-    side = 256
+    side = stride // 2
     me = lax.axis_index("state")
     part = lax.axis_index("mesh")
 
@@ -205,7 +205,7 @@
         lax.fori_loop(0, count // size, step, 0)
 
     pot[...] = jnp.zeros(pot.shape, f32)
-    pot[:, 0:nodes] = pot_ref[...]
+    pot[:, 0:nodes] = pot_ref[...].reshape(1, nodes)
     crow[...] = jnp.full(crow.shape, -1, jnp.int32)
     for cell in range(cells):
         crow[:, cell * stride : cell * stride + npc] = cells_ref[cell : cell + 1, :]
@@ -253,99 +253,134 @@
     begin(0, 1, 4)
 
     def rotate(phase, owner, total, fresh=False):
-        rh[...], rl[...] = split(rbuf[owner])
+        high, rest = split(rbuf[owner])
+        r3[0:half], r3[half : 2 * half], r3[2 * half :] = high, rest, high
 
         def body(rows):
             high, rest = split(g[phase, owner, rows, :])
-            value = dot3(high, rest, rh[...], rl[...])
+            value = dot(jnp.concatenate([high, high, rest], axis=1), r3[...])
             total[rows, :] = value if fresh else total[rows, :] + value
 
         tiles(n_pad, tile, body)
 
+    buffers = (
+        ((half_put_a, half_got_a, pair_a), (half_put_b, half_got_b, pair_b)),
+        ((put_a, got_a, pair_a), (put_b, got_b, pair_b)),
+    )
+
     def trade(field, number, which):
-        put, got, pair = ((put_a, got_a, pair_a), (put_b, got_b, pair_b))[which]
-        slot = 2 * field + number
+        put, got, pair = buffers[field][which]
         return pltpu.make_async_remote_copy(
-            src_ref=put.at[slot],
-            dst_ref=got.at[slot],
-            send_sem=e_send.at[which, slot],
-            recv_sem=e_recv.at[which, slot],
+            src_ref=put.at[number],
+            dst_ref=got.at[number],
+            send_sem=e_send.at[which, 2 * field + number],
+            recv_sem=e_recv.at[which, 2 * field + number],
             device_id={"mesh": pair},
             device_id_type=MESH,
         )
 
-    def enter(bank, read):
+    def hold(field, high_ref, rest_ref, rows, value):
+        high, rest = split(value)
+        if field:
+            high_ref[rows, :], rest_ref[rows, :] = high, rest
+        else:
+            high_ref[rows, 0:half], high_ref[rows, half:] = high, rest
+
+    def fold(value):
+        return value[:, 0:half] + value[:, half:]
+
+    def times(field, left, high_ref, rest_ref, rows):
+        if field:
+            return dot2(left, high_ref[rows, :], rest_ref[rows, :])
+        return fold(dot(left, high_ref[rows, :]))
+
+    def times_value(field, left, value):
+        high, rest = split(value)
+        if field:
+            return dot2(left, high, rest)
+        return fold(dot(left, jnp.concatenate([high, rest], axis=1)))
+
+    def width(field):
+        return slice(0, cols if field else half)
+
+    def enter(field, read):
         def split_body(rows):
-            ph[bank, rows, :], pl_[bank, rows, :] = split(read(rows))
+            hold(field, ph, pl_, rows, read(rows))
 
         tiles(n_pad, tile, split_body)
 
         def body(rows):
-            gh[bank, rows, :] = dot(pick[rows, :], ph[bank, 0:n_pad, :]).astype(bf16)
-            gl[bank, rows, :] = dot(pick[rows, :], pl_[bank, 0:n_pad, :]).astype(bf16)
+            gh[rows, :] = dot(pick[rows, :], ph[0:n_pad, :]).astype(bf16)
+            if field:
+                gl[rows, :] = dot(pick[rows, :], pl_[0:n_pad, :]).astype(bf16)
 
         tiles(cells * stride, side, body)
 
-    def product(bank, field, number):
+    def product(field, number):
         for cell in range(cells):
             span = slice(cell * stride, (cell + 1) * stride)
 
             def body(rows):
-                value = dot3(kh[rows, :], kl[rows, :], gh[bank, span, :], gl[bank, span, :])
                 here = pl.ds(pl.multiple_of(rows.start + cell * stride, 32), side)
-                ph[bank, here, :], pl_[bank, here, :] = split(value)
-                held = gh[bank, here, :].astype(f32) + gl[bank, here, :].astype(f32)
-                bv[bank, here, :] = value + dcol[here, :] * held
+                value = times(field, kh[rows, :], gh, gl, span)
+                value = value + dot(kl[rows, :], gh[span, width(field)])
+                hold(field, ph, pl_, here, value)
+                if field:
+                    held = gh[here, :].astype(f32) + gl[here, :].astype(f32)
+                else:
+                    held = fold(gh[here, :].astype(f32))
+                bv[here, width(field)] = value + dcol[here, :] * held
 
             tiles(stride, side, body)
-        slot = 2 * field + number
-        for put, col in ((put_a, near_col), (put_b, far_col)):
-            put[slot] = dot2(one_hot_used(col[...], crow[...]), ph[bank], pl_[bank])
-            if put is put_a:
+        every = slice(0, cells * stride)
+        for which, col in ((0, near_col), (1, far_col)):
+            picked = times(field, one_hot_used(col[...], crow[...]), ph, pl_, every)
+            buffers[field][which][0][number] = picked
+            if which == 0:
                 trade(field, number, 0).start()
 
-    def couple(bank):
+    def couple(field):
         for index, (one, two) in enumerate(pairs):
             span = slice(two * stride, (two + 1) * stride)
 
             def body(rows):
                 here = pl.ds(pl.multiple_of(rows.start + one * stride, 32), side)
-                value = dot2(same[index, rows, :], ph[bank, span, :], pl_[bank, span, :])
-                bv[bank, here, :] = bv[bank, here, :] + value
+                value = times(field, same[index, rows, :], ph, pl_, span)
+                bv[here, width(field)] = bv[here, width(field)] + value
 
             tiles(stride, side, body)
 
     def link(field, number):
-        slot = 2 * field + number
         trade(field, number, 0).wait_recv()
         corner = one_hot_used(far_col[...], near_row[:, 0 : near_col.shape[0]])
-        put_b[slot] = put_b[slot] + dot2(corner, *split(got_a[slot]))
+        got, put = buffers[field][0][1], buffers[field][1][0]
+        put[number] = put[number] + times_value(field, corner, got[number])
         trade(field, number, 1).start()
 
-    def finish(bank, field, number):
-        slot = 2 * field + number
+    def finish(field, number):
         trade(field, number, 1).wait_recv()
-        near_high, near_rest = split(got_a[slot])
-        far_high, far_rest = split(got_b[slot])
+        near_got, far_got = buffers[field][0][1], buffers[field][1][1]
 
         def body(rows):
             near = one_hot_used(ccol[rows, :], near_row[:, 0 : near_col.shape[0]])
             far = one_hot_used(ccol[rows, :], far_row[:, 0 : far_col.shape[0]])
-            value = bv[bank, rows, :] + dot2(near, near_high, near_rest)
-            value = value + dot2(far, far_high, far_rest)
-            gh[bank, rows, :], gl[bank, rows, :] = split(value * (1.0 / half_width))
+            value = bv[rows, width(field)] + times_value(field, near, near_got[number])
+            value = value + times_value(field, far, far_got[number])
+            hold(field, gh, gl, rows, value * (1.0 / half_width))
 
         tiles(cells * stride, side, body)
 
-    def leave(bank, write):
+    def leave(field, write):
+        size = tile // 2
+
         def body(rows):
-            ids = lax.broadcasted_iota(jnp.int32, (tile, crep.shape[1]), 0) + rows.start
-            write(rows, dot2(one_hot(ids, crep[...]), gh[bank], gl[bank]))
-
-        tiles(n_pad, tile, body)
+            ids = lax.broadcasted_iota(jnp.int32, (size, crep.shape[1]), 0) + rows.start
+            write(rows, times(field, one_hot(ids, crep[...]), gh, gl, slice(0, cells * stride)))
+
+        tiles(n_pad, size, body)
 
     enter(0, lambda rows: g[1, me, rows, :])
-    product(0, 0, 0)
+    product(0, 0)
     couple(0)
     for copy in rotation_copies:
         copy.wait()
@@ -353,20 +388,20 @@
     link(0, 0)
     arrived(0, 6)
     rotate(0, sib, c1)
-    finish(0, 0, 0)
-    product(0, 0, 1)
+    finish(0, 0)
+    product(0, 1)
     couple(0)
     pass_first(0)
     link(0, 1)
-    finish(0, 0, 1)
+    pass_second(0)
+    rotate(0, xs, c1)
+    finish(0, 1)
 
     def leave_half(rows, value):
         g[1, me, rows, :] = 2.0 * value - g[1, me, rows, :]
 
     leave(0, leave_half)
     begin(1, 0, 3, 6)
-    pass_second(0)
-    rotate(0, xs, c1)
     rotate(0, ys, c1)
     arrived(0, 7, 8)
     rotate(0, flip(xs, 1), c1)
@@ -380,37 +415,29 @@
     rotation_copies = load_rotation(1)
     c1[pl.ds(n_send, n_pad - n_send), :] = jnp.zeros((n_pad - n_send, cols), f32)
 
-    spans = [slice(0, half), slice(half, cols)]
-
-    for bank in range(2):
-        enter(bank, lambda rows: c1[rows, spans[bank]])
-        product(bank, bank + 1, 0)
-    for bank in range(2):
-        couple(bank)
-        link(bank + 1, 0)
+    enter(1, lambda rows: c1[rows, :])
+    product(1, 0)
+    couple(1)
     for copy in rotation_copies:
         copy.wait()
     rotate(1, me, out_ref, fresh=True)
+    link(1, 0)
     pass_first(1)
-    for bank in range(2):
-        finish(bank, bank + 1, 0)
-        product(bank, bank + 1, 1)
-    for bank in range(2):
-        couple(bank)
-        link(bank + 1, 1)
     arrived(1, 6)
     rotate(1, sib, out_ref)
+    finish(1, 0)
+    product(1, 1)
+    couple(1)
+    link(1, 1)
     pass_second(1)
-    for bank in range(2):
-        finish(bank, bank + 1, 1)
-
-        def leave_whole(rows, value):
-            span = spans[bank]
-            out_ref[rows, span] = out_ref[rows, span] + (2.0 * value - c1[rows, span])
-
-        leave(bank, leave_whole)
     rotate(1, xs, out_ref)
     rotate(1, ys, out_ref)
+    finish(1, 1)
+
+    def leave_whole(rows, value):
+        out_ref[rows, :] = out_ref[rows, :] + (2.0 * value - c1[rows, :])
+
+    leave(1, leave_whole)
     pass_third(1)
     arrived(1, 7, 8)
     rotate(1, flip(xs, 1), out_ref)
@@ -422,7 +449,7 @@
     for moves in plans:
         for move in moves:
             move.wait_send()
-    for field in range(3):
+    for field in range(2):
         for number in range(2):
             for which in range(2):
                 trade(field, number, which).wait_send()
@@ -449,13 +476,12 @@
         pltpu.VMEM((stride, stride), bf16),
         pltpu.VMEM((cells * stride, n_pad), bf16),
         pltpu.VMEM((cells * (cells - 1), stride, stride), bf16),
-        pltpu.VMEM((2, cells * stride, half), bf16),
-        pltpu.VMEM((2, cells * stride, half), bf16),
-        pltpu.VMEM((2, cells * stride, half), bf16),
-        pltpu.VMEM((2, cells * stride, half), bf16),
-        pltpu.VMEM((2, cells * stride, half), f32),
-        pltpu.VMEM((half, cols), bf16),
-        pltpu.VMEM((half, cols), bf16),
+        pltpu.VMEM((cells * stride, cols), bf16),
+        pltpu.VMEM((cells * stride, cols), bf16),
+        pltpu.VMEM((cells * stride, cols), bf16),
+        pltpu.VMEM((cells * stride, cols), bf16),
+        pltpu.VMEM((cells * stride, cols), f32),
+        pltpu.VMEM((3 * half, cols), bf16),
         pltpu.VMEM((1, n_pad), f32),
         pltpu.VMEM((1, cells * stride), jnp.int32),
         pltpu.VMEM((1, cells * stride), jnp.int32),
@@ -465,14 +491,18 @@
         pltpu.VMEM((1, up(far, 128)), jnp.int32),
         pltpu.VMEM((near, 1), jnp.int32),
         pltpu.VMEM((far, 1), jnp.int32),
-        pltpu.VMEM((6, near, half), f32),
-        pltpu.VMEM((6, near, half), f32),
-        pltpu.VMEM((6, far, half), f32),
-        pltpu.VMEM((6, far, half), f32),
+        pltpu.VMEM((2, near, half), f32),
+        pltpu.VMEM((2, near, half), f32),
+        pltpu.VMEM((2, far, half), f32),
+        pltpu.VMEM((2, far, half), f32),
+        pltpu.VMEM((2, near, cols), f32),
+        pltpu.VMEM((2, near, cols), f32),
+        pltpu.VMEM((2, far, cols), f32),
+        pltpu.VMEM((2, far, cols), f32),
         pltpu.SemaphoreType.DMA((2, 13)),
         pltpu.SemaphoreType.DMA((2, 13)),
-        pltpu.SemaphoreType.DMA((2, 6)),
-        pltpu.SemaphoreType.DMA((2, 6)),
+        pltpu.SemaphoreType.DMA((2, 4)),
+        pltpu.SemaphoreType.DMA((2, 4)),
         pltpu.SemaphoreType.DMA((blocks,)),
     ]
     padded = pl.pallas_call(
@@ -485,7 +515,7 @@
             collective_id=0, has_side_effects=True, vmem_limit_bytes=64 * 1024 * 1024
         ),
     )(
-        states_in, rotation, stiffness, potential[None, :], cell_nodes, shared_rows, shared_count
+        states_in, rotation, stiffness, potential, cell_nodes, shared_rows, shared_count
     )
     return padded[:nodes]
 

time: 140 us -> 139 us (level)
  no operation moved by 1% of the time
where the time goes in v1:
time: 139 us
  Pallas kernels  132 us (95%)
  local copies, waits for them, and re-layouts  6.78 us (5%)
    pallas_call x1, Pallas kernels, square_device(): pl.pallas_call(functools.partial(kernel, grid_side, near_rows, far_rows),...  132 us
    slice x1, local copies, waits for them, and re-layouts, square_device(): return padded[:nodes]  3.63 us
    unnamed x1, local copies, waits for them, and re-layouts  3.15 us

profile of v1, /device:TPU:0, one launch (start us, length us, event | category | flops | bytes accessed | tf_op | source)
XLA Modules:
  0.0 138.7 jit_solution(10497142898778442476)
XLA Ops:
  0.0 3.1 %copy.8.k_ref = f32[1,729,729]{2,1,0:T(8,128)} copy(f32[1,729,729]{2,0,1:T(1,128)} %param.9) | data formatting | bytes 4251528 | tf_op args[2]
  3.2 131.9 %shard_map.73 = f32[1408,512]{1,0:T(8,128)} custom-call(f32[1377,512]{1,0:T(8,128)} %x_ref.1, f32[4096,512]{1,0:T(8,128)} %rot_ref.1, f32[1,729,729]{2,1,0:T(8,128)} %copy.8.k_ref, f32[1377]{0:T(1024)} %pot_ref.1, s32[2,729]{1,0:T(2,128)} %cells_ref.1, s32[4,153]{1,0:T(4,128)} %lists_ref.1, s32[1,4]{1,0:T(1,128)} %count_ref.1), custom_call_target="tpu_custom_call" | custom-call | tf_op jit(solution)/shard_map/pallas_call | solution.py:508
  135.1 3.6 %slice.3 = f32[1377,512]{1,0:T(8,128)} slice(f32[1408,512]{1,0:T(8,128)} %shard_map.73), slice={[0:1377], [0:512]} | slice | bytes 5640192 | tf_op jit(solution)/shard_map/slice | solution.py:520

commit v2 on v1

--- a/solution.py
+++ b/solution.py
@@ -98,7 +98,7 @@
     g, rbuf, c1, kh, kl, pick, same, gh, gl, ph, pl_, bv, r3,
     pot, crow, crep, ccol, dcol, near_row, far_row, near_col, far_col,
     half_put_a, half_got_a, half_put_b, half_got_b, put_a, got_a, put_b, got_b,
-    g_send, g_recv, e_send, e_recv, r_sem,
+    k_held, g_send, g_recv, e_send, e_recv, r_sem, k_sem,
 ):
     nodes = x_ref.shape[0]
     n_pad, cols = c1.shape
@@ -135,11 +135,13 @@
             copies.append(copy)
         return copies
 
-    rotation_copies = load_rotation(0)
     last = nodes // 8 * 8
-    for phase in range(2):
+
+    def take(phase):
         g[phase, me, pl.ds(last, n_pad - last), :] = jnp.zeros((n_pad - last, half), f32)
         g[phase, me, pl.ds(0, nodes), :] = x_ref[:, phase * half : (phase + 1) * half]
+
+    take(0)
     pl.semaphore_wait(barrier, 5)
 
     def send(phase, number, owner, rows, target):
@@ -196,6 +198,10 @@
             plans[phase][number].wait_recv()
 
     begin(0, 0, 3, 6)
+    k_copy = pltpu.make_async_copy(k_ref, k_held, k_sem.at[0])
+    k_copy.start()
+    rotation_copies = load_rotation(0)
+    take(1)
 
     def tiles(count, size, body):
         def step(index, carry):
@@ -224,11 +230,12 @@
     far_col[...] = to_column(far_row[...])[0 : far_col.shape[0]]
     ccol[...] = to_column(crow[...])
 
+    k_copy.wait()
     for first in range(0, stride, cols):
         width = min(cols, stride - first)
         used = min(npc - first, width)
         out_ref[0:stride, 0:width] = jnp.zeros((stride, width), f32)
-        out_ref[0:npc, 0:used] = k_ref[0, :, first : first + used]
+        out_ref[0:npc, 0:used] = k_held[:, 0, first : first + used]
         span = slice(first, first + width)
         kh[:, span], kl[:, span] = split(out_ref[0:stride, 0:width])
 
@@ -408,7 +415,6 @@
     arrived(0, 9, 10)
     rotate(0, flip(ys, 1), c1)
     pass_third(0)
-    begin(1, 1, 4)
     rotate(0, ds, c1)
     arrived(0, 11, 12)
     rotate(0, flip(ds, 1), c1)
@@ -416,6 +422,7 @@
     c1[pl.ds(n_send, n_pad - n_send), :] = jnp.zeros((n_pad - n_send, cols), f32)
 
     enter(1, lambda rows: c1[rows, :])
+    begin(1, 1, 4)
     product(1, 0)
     couple(1)
     for copy in rotation_copies:
@@ -438,11 +445,11 @@
         out_ref[rows, :] = out_ref[rows, :] + (2.0 * value - c1[rows, :])
 
     leave(1, leave_whole)
-    pass_third(1)
     arrived(1, 7, 8)
     rotate(1, flip(xs, 1), out_ref)
     arrived(1, 9, 10)
     rotate(1, flip(ys, 1), out_ref)
+    pass_third(1)
     rotate(1, ds, out_ref)
     arrived(1, 11, 12)
     rotate(1, flip(ds, 1), out_ref)
@@ -468,6 +475,7 @@
     grid_side = math.isqrt(lax.axis_size("mesh"))
     vmem = pl.BlockSpec(memory_space=pltpu.VMEM)
     smem = pl.BlockSpec(memory_space=pltpu.SMEM)
+    held = pl.BlockSpec(memory_space=pl.ANY)
     scratch = [
         pltpu.VMEM((2, blocks, n_pad, half), f32),
         pltpu.VMEM((blocks, half, cols), f32),
@@ -499,23 +507,31 @@
         pltpu.VMEM((2, near, cols), f32),
         pltpu.VMEM((2, far, cols), f32),
         pltpu.VMEM((2, far, cols), f32),
+        pltpu.VMEM((npc, 1, npc), f32),
         pltpu.SemaphoreType.DMA((2, 13)),
         pltpu.SemaphoreType.DMA((2, 13)),
         pltpu.SemaphoreType.DMA((2, 4)),
         pltpu.SemaphoreType.DMA((2, 4)),
         pltpu.SemaphoreType.DMA((blocks,)),
+        pltpu.SemaphoreType.DMA((1,)),
     ]
     padded = pl.pallas_call(
         functools.partial(kernel, grid_side, near_rows, far_rows),
         out_shape=jax.ShapeDtypeStruct((n_pad, cols), f32),
-        in_specs=[vmem, pl.BlockSpec(memory_space=pl.ANY), vmem, vmem, vmem, vmem, smem],
+        in_specs=[vmem, held, held, vmem, vmem, vmem, smem],
         out_specs=vmem,
         scratch_shapes=scratch,
         compiler_params=pltpu.CompilerParams(
             collective_id=0, has_side_effects=True, vmem_limit_bytes=64 * 1024 * 1024
         ),
     )(
-        states_in, rotation, stiffness, potential, cell_nodes, shared_rows, shared_count
+        states_in,
+        rotation,
+        jnp.transpose(stiffness, (1, 0, 2)),
+        potential,
+        cell_nodes,
+        shared_rows,
+        shared_count,
     )
     return padded[:nodes]
 

time: 139 us -> 137 us (0.986)
  local copies, waits for them, and re-layouts: 6.78 us -> 3.63 us
    unnamed x1 -> x0, local copies, waits for them, and re-layouts: 3.15 us -> none
where the time goes in v2:
time: 137 us; the launch traced here: 136 us
  Pallas kernels  133 us (97%)
  local copies, waits for them, and re-layouts  3.63 us (3%)
    pallas_call x1, Pallas kernels, square_device(): pl.pallas_call(functools.partial(kernel, grid_side, near_rows, far_rows),...  133 us
    slice x1, local copies, waits for them, and re-layouts, square_device(): return padded[:nodes]  3.63 us

profile of v2, /device:TPU:0, one launch (start us, length us, event | category | flops | bytes accessed | tf_op | source)
XLA Modules:
  0.0 136.3 jit_solution(13580749961951444964)
XLA Ops:
  0.0 132.6 %shard_map.73 = f32[1408,512]{1,0:T(8,128)} custom-call(f32[1377,512]{1,0:T(8,128)} %x_ref.1, f32[4096,512]{1,0:T(8,128)} %rot_ref.1, f32[729,1,729]{2,1,0:T(1,128)} %bitcast.1, f32[1377]{0:T(1024)} %pot_ref.1, s32[2,729]{1,0:T(2,128)} %cells_ref.1, s32[4,153]{1,0:T(4,128)} %lists_ref.1, s32[1,4]{1,0:T(1,128)} %count_ref.1), custom_call_target="tpu_custom_call" | custom-call | tf_op jit(solution)/shard_map/pallas_call | solution.py:518
  132.6 3.6 %slice.3 = f32[1377,512]{1,0:T(8,128)} slice(f32[1408,512]{1,0:T(8,128)} %shard_map.73), slice={[0:1377], [0:512]} | slice | bytes 5640192 | tf_op jit(solution)/shard_map/slice | solution.py:536

commit v3 on v2

--- a/solution.py
+++ b/solution.py
@@ -125,15 +125,14 @@
     for target in ({"state": sib}, {"state": xs}, {"state": ys}, {"mesh": pair_a}, {"mesh": pair_b}):
         pl.semaphore_signal(barrier, inc=1, device_id=target, device_id_type=MESH)
 
+    def load_block(phase, block):
+        rows = pl.ds(pl.multiple_of(block * cols + phase * half, half), half)
+        copy = pltpu.make_async_copy(rot_ref.at[rows], rbuf.at[block], r_sem.at[block])
+        copy.start()
+        return copy
+
     def load_rotation(phase):
-        copies = []
-        for block in range(rbuf.shape[0]):
-            copy = pltpu.make_async_copy(
-                rot_ref.at[pl.ds(block * cols + phase * half, half)], rbuf.at[block], r_sem.at[block]
-            )
-            copy.start()
-            copies.append(copy)
-        return copies
+        return [load_block(phase, block) for block in range(rbuf.shape[0])]
 
     last = nodes // 8 * 8
 
@@ -392,6 +391,7 @@
     for copy in rotation_copies:
         copy.wait()
     rotate(0, me, c1, fresh=True)
+    own_copy = load_block(1, me)
     link(0, 0)
     arrived(0, 6)
     rotate(0, sib, c1)
@@ -408,13 +408,16 @@
         g[1, me, rows, :] = 2.0 * value - g[1, me, rows, :]
 
     leave(0, leave_half)
-    begin(1, 0, 3, 6)
+    begin(1, 6)
     rotate(0, ys, c1)
     arrived(0, 7, 8)
     rotate(0, flip(xs, 1), c1)
     arrived(0, 9, 10)
     rotate(0, flip(ys, 1), c1)
+    own_copy.wait()
+    rotate(1, me, out_ref, fresh=True)
     pass_third(0)
+    begin(1, 0, 3)
     rotate(0, ds, c1)
     arrived(0, 11, 12)
     rotate(0, flip(ds, 1), c1)
@@ -422,18 +425,17 @@
     c1[pl.ds(n_send, n_pad - n_send), :] = jnp.zeros((n_pad - n_send, cols), f32)
 
     enter(1, lambda rows: c1[rows, :])
+    product(1, 0)
     begin(1, 1, 4)
-    product(1, 0)
     couple(1)
     for copy in rotation_copies:
         copy.wait()
-    rotate(1, me, out_ref, fresh=True)
     link(1, 0)
-    pass_first(1)
     arrived(1, 6)
     rotate(1, sib, out_ref)
     finish(1, 0)
     product(1, 1)
+    pass_first(1)
     couple(1)
     link(1, 1)
     pass_second(1)

time: 137 us -> 138 us (level)
  no operation moved by 1% of the time
where the time goes in v3:
time: 138 us; the launch traced here: 137 us
  Pallas kernels  133 us (96%)
  local copies, waits for them, and re-layouts  3.63 us (3%)
    pallas_call x1, Pallas kernels, square_device(): pl.pallas_call(functools.partial(kernel, grid_side, near_rows, far_rows),...  133 us
    slice x1, local copies, waits for them, and re-layouts, square_device(): return padded[:nodes]  3.63 us

profile of v3, /device:TPU:0, one launch (start us, length us, event | category | flops | bytes accessed | tf_op | source)
XLA Modules:
  0.0 136.9 jit_solution(18103301802935882129)
XLA Ops:
  0.0 133.3 %shard_map.73 = f32[1408,512]{1,0:T(8,128)} custom-call(f32[1377,512]{1,0:T(8,128)} %x_ref.1, f32[4096,512]{1,0:T(8,128)} %rot_ref.1, f32[729,1,729]{2,1,0:T(1,128)} %bitcast.1, f32[1377]{0:T(1024)} %pot_ref.1, s32[2,729]{1,0:T(2,128)} %cells_ref.1, s32[4,153]{1,0:T(4,128)} %lists_ref.1, s32[1,4]{1,0:T(1,128)} %count_ref.1), custom_call_target="tpu_custom_call" | custom-call | tf_op jit(solution)/shard_map/pallas_call | solution.py:520
  133.3 3.6 %slice.3 = f32[1377,512]{1,0:T(8,128)} slice(f32[1408,512]{1,0:T(8,128)} %shard_map.73), slice={[0:1377], [0:512]} | slice | bytes 5640192 | tf_op jit(solution)/shard_map/slice | solution.py:538
